TPU v7x, 128 devices: a whole 4x4x4 slice. The times are simulated.
128 devices in a mesh: grp: 4 (over x_hi, core), tile: 32 (over x_lo, y, z).
Axes of the slice: x: 4 (x_hi: 2, x_lo: 2; x = x_hi * 2 + x_lo), y: 4, z: 4, core: 2. Of those that a mesh axis runs over, the one named last changes fastest.
Arguments:
- start_field: float32 [512, 512, 512], P('grp', 'tile'), may hold values from -4 to 4
- class_ids: int32 [512, 512], P('tile'), may hold values from 0 to 7
- run_levels: int32 [512, 8], replicated, may hold values from 0 to 7
- steepness: float32 [512], replicated, may hold values from 0.1 to 1
- step_pick: int32 [512], replicated, may hold values from 1 to 4
- input_layer: float32 [69, 2048], replicated, may hold values from -2 to 2
- output_layer: bfloat16 [2048, 262144], P(None, ('grp', 'tile')), may hold values from -0.125 to 0.125
- output_bias: float32 [262144], P(('grp', 'tile')), may hold values from -1.5 to 1.5
Outputs:
- misfit: bfloat16 [512, 262144], P(None, ('grp', 'tile'))
- output_next: bfloat16 [2048, 262144], P(None, ('grp', 'tile'))
- bias_next: float32 [262144], P(('grp', 'tile'))
- input_next: float32 [69, 2048], replicated
All inputs are finite; a program needn't handle non-finite values.
Results may differ from a plain program's by a relative error of at most 0.0029.
The roundings to bfloat16 on the way count: a program that leaves them out, or rounds other values in their place, can miss the bound.
Values sent between devices are 32-bit elements; how exact they have to be, the bound alone decides.
A program may use at most 128 MiB of HBM per device.

v0:
```python
import jax
import jax.numpy as jnp
from jax import lax
from jax.sharding import Mesh
from jax.sharding import PartitionSpec as P

STEPS = 4
LEVELS = 8
GRP = ("grp_0", "grp_1")
GRP_TILE = ("grp_0", "grp_1", "tile")


def with_halo(value, sides, width):
    for axis, dim in sides:
        size, length = (lax.axis_size(axis), value.shape[dim])
        up = [(i, (i + 1) % size) for i in range(size - 1)]
        down = [(j, i) for i, j in up]
        last = lax.slice_in_dim(value, length - width, length, axis=dim)
        initial = lax.slice_in_dim(value, 0, width, axis=dim)
        before = lax.ppermute(last, axis, up)
        after = lax.ppermute(initial, axis, down)
        value = jnp.concatenate([before, value, after], axis=dim)
    return value


def in_blocks(value, dim, length):
    shape = value.shape
    tiles = value.reshape(*shape[:dim], length, shape[dim] // length, *shape[dim + 1 :])
    return jnp.moveaxis(tiles, dim, 0)


def in_order(tiles, dim):
    tiles = jnp.moveaxis(tiles, 0, dim)
    shape = tiles.shape
    return tiles.reshape(*shape[:dim], shape[dim] * shape[dim + 1], *shape[dim + 2 :])


def turned_blocks(tiles, axes, order):
    inside = tiles.shape[1:]
    out = tiles.reshape(*(lax.axis_size(a) for a in axes), *inside)
    for k in order:
        out = lax.all_to_all(out, axes[k], k, k, tiled=True)
    return out.reshape(-1, *inside)


def core_and_chips(value, groups, order, split_dim, concat_dim):
    length = lax.axis_size(groups[0]) * lax.axis_size(groups[1])
    tiles = in_blocks(value, split_dim, length)
    return in_order(turned_blocks(tiles, groups, order), concat_dim)


def coefficients(run_levels, class_ids):
    table = 0.03 * jnp.exp(run_levels.astype(jnp.float32) * jnp.log(jnp.float32(1.35)))
    kappa = jnp.zeros((run_levels.shape[0],) + class_ids.shape, jnp.float32)
    for klass in range(run_levels.shape[1]):
        picked = jnp.where(class_ids == klass, 1.0, 0.0).astype(jnp.float32)
        kappa = kappa + picked[None] * table[:, klass][:, None, None]
    return kappa


def advance(field, kappa, steep):
    ratio = field * field
    spread = kappa * (1.0 + steep * ratio) / (1.0 + ratio)
    fpad = jnp.pad(field, ((0, 0), (0, 0), (1, 1)))
    spad = jnp.pad(spread, ((0, 0), (0, 0), (1, 1)))
    centre = field[:, 1:-1]
    middle = spread[:, 1:-1]
    total = centre + 0.5 * (middle + spread[:, :-2]) * (field[:, :-2] - centre)
    total = total + 0.5 * (middle + spread[:, 2:]) * (field[:, 2:] - centre)
    total = total + 0.5 * (middle + spad[:, 1:-1, :-2]) * (fpad[:, 1:-1, :-2] - centre)
    total = total + 0.5 * (middle + spad[:, 1:-1, 2:]) * (fpad[:, 1:-1, 2:] - centre)
    return total


def features(run_levels, step_pick, steepness):
    count = run_levels.shape[0]
    onehot = (run_levels[:, :, None] == jnp.arange(LEVELS, dtype=jnp.int32)[None, None, :]).astype(
        jnp.float32
    )
    onehot = onehot.reshape(count, -1)
    moment = (step_pick[:, None] == jnp.arange(1, STEPS + 1, dtype=jnp.int32)[None, :]).astype(
        jnp.float32
    )
    return jnp.concatenate([onehot, moment, steepness[:, None]], axis=1)


def dsilu(pre):
    logistic = jax.nn.sigmoid(pre)
    return logistic * (1.0 + pre * (1.0 - logistic))


def on_device(
    start_field, class_ids, run_levels, steepness, step_pick, input_layer, output_layer, output_bias
):
    local_runs, rows, columns = start_field.shape
    first_run = lax.axis_index(GRP) * local_runs
    levels_here = lax.dynamic_slice_in_dim(run_levels, first_run, local_runs, 0)
    steep = lax.dynamic_slice_in_dim(steepness, first_run, local_runs, 0)[:, None, None]
    pick_here = lax.dynamic_slice_in_dim(step_pick, first_run, local_runs, 0)[:, None, None]
    snapshot = jnp.zeros_like(start_field)
    class_wide = with_halo(class_ids + 1, (("tile", 0),), STEPS)
    kappa_wide = coefficients(levels_here, class_wide - 1)
    wide = with_halo(start_field, (("tile", 1),), STEPS)
    first_row = lax.axis_index("tile") * rows - STEPS
    total_rows = rows * lax.axis_size("tile")
    span = kappa_wide.shape[1]
    for step in range(STEPS):
        margin = STEPS - step - 1
        kappa_now = kappa_wide[:, step : span - step]
        wide = advance(wide, kappa_now, steep)
        row_ids = first_row + step + 1 + jnp.arange(wide.shape[1], dtype=jnp.int32)
        inside = (row_ids >= 0) & (row_ids < total_rows)
        wide = jnp.where(inside[None, :, None], wide, 0.0)
        snapshot = jnp.where(pick_here == step + 1, wide[:, margin : margin + rows], snapshot)
    flat = snapshot.reshape(local_runs, rows * columns)
    target = core_and_chips(flat, ("grp_0", "grp_1"), (0, 1), 1, 0)
    runs_total = target.shape[0]
    feats = features(run_levels, step_pick, steepness)
    pre = jnp.dot(feats, input_layer, precision=lax.Precision.HIGHEST)
    hidden = jax.nn.silu(pre).astype(jnp.bfloat16)
    error = (
        jnp.dot(hidden, output_layer, preferred_element_type=jnp.float32)
        + output_bias[None, :]
        - target
    )
    slope = (error * (2.0 / runs_total)).astype(jnp.bfloat16)
    grad = lax.dot_general(
        hidden, slope, (((0,), (0,)), ((), ())), preferred_element_type=jnp.float32
    )
    output_next = (output_layer.astype(jnp.float32) - 0.5 * grad).astype(jnp.bfloat16)
    bias_next = output_bias - 0.5 * jnp.sum(slope.astype(jnp.float32), axis=0)
    gain_slope = dsilu(pre)
    partial_back = lax.dot_general(
        slope, output_layer, (((1,), (1,)), ((), ())), preferred_element_type=jnp.float32
    )
    partial_in = lax.dot_general(
        feats, partial_back * gain_slope, (((0,), (0,)), ((), ())), precision=lax.Precision.HIGHEST
    )
    grad_in = lax.psum(partial_in, GRP_TILE)
    input_next = input_layer - 2.0 * grad_in
    return (error.astype(jnp.bfloat16), output_next, bias_next, input_next)


def solution(mesh):
    split = Mesh(mesh.devices.reshape(2, 2, mesh.shape["tile"]), ("grp_0", "grp_1", "tile"))
    return jax.shard_map(
        on_device,
        mesh=split,
        in_specs=(
            P(GRP, "tile", None),
            P("tile", None),
            P(),
            P(),
            P(),
            P(),
            P(None, GRP_TILE),
            P(GRP_TILE),
        ),
        out_specs=(P(None, GRP_TILE), P(None, GRP_TILE), P(GRP_TILE), P()),
        check_vma=False,
    )
```

profile of v0, /device:TPU:1, one launch (start us, length us, event | category | flops | bytes accessed | tf_op | source)
XLA Modules:
  0.0 382.8 jit_solution(13823181372475220173)
XLA Ops:
  7.2 0.8 broadcast_add_fusion
  8.0 4.4 %collective-permute-start.2 = (s32[4,512]{1,0:T(4,128)S(1)}, s32[4,512]{1,0:T(4,128)S(1)}, u32[]{:S(2)}, u32[]{:S(2)}) collective-permute-start(s32[4,512]{1,0:T(4,128)S(1)} %get-tuple-element.24), channel_id=1, source_target_pairs={{0,1},{1,2},{2,3},{3,4},{4,5},{5,6},{6,7},{7,8},{8,9},{9,10},{10,1... | collective-permute-start | bytes 24584 | tf_op jit(solution)/shard_map/ppermute | solution.py:20
  12.3 1.3 collective-permute-start.3
  13.6 2.7 fusion.90
  16.7 4.2 %collective-permute-start = (f32[128,4,512]{2,0,1:T(8,128)S(1)}, f32[128,4,512]{2,0,1:T(8,128)S(1)}, u32[]{:S(2)}, u32[]{:S(2)}) collective-permute-start(f32[128,4,512]{2,0,1:T(8,128)S(1)} %copy.34), channel_id=1, source_target_pairs={{0,1},{1,2},{2,3},{3,4},{4,5},{5,6},{6,7},{7,8},{8,9},{9,10},{10,1... | collective-permute-start | bytes 3145736 | tf_op jit(solution)/shard_map/ppermute | solution.py:20
  21.0 1.3 copy.35
  22.3 1.3 collective-permute-start.1
  25.4 1.3 broadcast_compare_fusion.3
  27.8 5.3 %copy.29 = f32[128,16,512]{0,2,1:T(8,128)} copy(f32[128,16,512]{2,1,0:T(8,128)} %param.8) | data formatting | bytes 8388608 | tf_op args[0]
  33.1 0.8 dynamic_slice.11
  34.0 14.8 %multiply_add_fusion = f32[128,24,512]{0,2,1:T(8,128)} fusion(f32[128]{0:T(128)S(1)} %get-tuple-element.27, f32[24,512]{1,0:T(8,128)S(1)} %get-tuple-element.23, f32[128]{0:T(128)S(1)} %get-tuple-element.28, f32[24,512]{1,0:T(8,128)S(1)} %get-tuple-element.22, f32[128]{0:T(128)S(1)} %get-tuple-element.29, f32[24,512]{1,0:T(8,128)S(1)} %get-tuple-element.21, ...), kind=kLoop, calls=%fused_computation.3 | loop fusion | flops 23592960 | bytes 6688768 | tf_op jit(solution)/shard_map/add | solution.py:57
  49.3 1.5 copy.30
  50.9 1.0 copy-done.3
  52.0 2.7 pad_maximum_fusion
  55.4 15.7 %add_divide_fusion = f32[128,24,512]{0,2,1:T(8,128)S(1)} fusion(f32[128]{0:T(128)S(1)} %dynamic_slice.11, f32[128,4,512]{0,2,1:T(8,128)} %copy-done.3, f32[128,16,512]{0,2,1:T(8,128)S(1)} %copy-done.2, f32[128,4,512]{0,2,1:T(8,128)S(1)} %copy.28, f32[128]{0:T(128)S(1)} %copy-done.25, f32[24,512]{1,0:T(8,128)S(1)} %copy-done.9, f32[128]{0:T(128)S(1)} %copy-done.27, ...), kind=kLoop, calls=%fused_computation.2 | loop fusion | flops 36175872 | bytes 12980736 | tf_op jit(solution)/shard_map/div | solution.py:63
  71.1 11.3 %fusion.11 = (f32[128,22,512]{0,2,1:T(8,128)}, f32[128,22,512]{0,2,1:T(8,128)S(1)}) fusion(f32[128,24,512]{0,2,1:T(8,128)} %multiply_add_fusion, f32[128]{0:T(128)S(1)} %dynamic_slice.11, f32[128,24,512]{0,2,1:T(8,128)S(1)} %pad_maximum_fusion, f32[128,24,512]{0,2,1:T(8,128)S(1)} %add_divide_fusion, pred[22]{0:T(512)(128)(4,1)} %compare_and_fusion), kind=kLoop, calls=%fused_computation.20 | loop fusion | flops 38928384 | bytes 64487960 | tf_op jit(solution)/shard_map/div | solution.py:63
  82.4 16.6 %fusion.29 = (f32[128,20,512]{0,2,1:T(8,128)S(1)}, f32[128,20,512]{0,2,1:T(8,128)S(1)}) fusion(f32[128,24,512]{0,2,1:T(8,128)} %multiply_add_fusion, f32[128]{0:T(128)S(1)} %dynamic_slice.11, f32[128,22,512]{0,2,1:T(8,128)S(1)} %get-tuple-element.11, f32[128,22,512]{0,2,1:T(8,128)} %get-tuple-element.10, pred[20]{0:T(512)(128)(4,1)S(1)} %copy-done.46), kind=kLoop, calls=%fused_computation.47 | loop fusion | flops 35389440 | bytes 58721280 | tf_op jit(solution)/shard_map/div | solution.py:63
  99.1 10.9 %fusion.47 = (f32[128,18,512]{0,2,1:T(8,128)}, f32[128,18,512]{0,2,1:T(8,128)}) fusion(f32[128,24,512]{0,2,1:T(8,128)} %multiply_add_fusion, f32[128]{0:T(128)S(1)} %dynamic_slice.11, f32[128,20,512]{0,2,1:T(8,128)S(1)} %get-tuple-element.9, f32[128,20,512]{0,2,1:T(8,128)S(1)} %get-tuple-element.8, pred[18]{0:T(512)(128)(4,1)S(1)} %copy-done.45), kind=kLoop, calls=%fused_computation.74 | loop fusion | flops 31850496 | bytes 52954112 | tf_op jit(solution)/shard_map/div | solution.py:63
  110.0 21.7 %fusion.60 = f32[128,16,512]{0,2,1:T(8,128)} fusion(f32[128,18,512]{0,2,1:T(8,128)} %get-tuple-element.6, f32[128,18,512]{0,2,1:T(8,128)} %get-tuple-element.7, f32[128,22,512]{0,2,1:T(8,128)} %copy-done, f32[128,20,512]{0,2,1:T(8,128)} %copy-done.1, pred[16]{0:T(512)(128)(4,1)S(1)} %copy-done.44, pred[128]{0:T(512)(128)(4,1)S(1)} %copy-done.43, ...), kind=kLoop, calls=%fused_computation.95 | loop fusion | flops 26214400 | bytes 47186448 | tf_op jit(solution)/shard_map/jit(_where)/select_n | solution.py:114
  131.7 5.6 %copy.31 = f32[4,128,2048]{2,1,0:T(8,128)} copy(f32[4,128,2048]{1,2,0:T(8,128)} %bitcast.30) | data formatting | bytes 8388608 | tf_op jit(solution)/shard_map/transpose | solution.py:29
  137.3 5.8 %all-to-all-start = ((f32[2,2,128,2048]{3,2,1,0:T(8,128)}), f32[2,2,128,2048]{3,2,1,0:T(8,128)}, u32[]{:S(2)}, u32[]{:S(2)}) async-start(f32[2,2,128,2048]{3,2,1,0:T(8,128)} %bitcast.31), calls=%async_computation | async-start | bytes 8388608 | tf_op jit(solution)/shard_map/all_to_all | solution.py:42
  143.4 5.1 %fusion.82 = f32[512,2048]{1,0:T(8,128)} fusion(f32[69,2048]{1,0:T(8,128)S(1)} %copy-done.5, f32[512,1]{0,1:T(1,128)S(1)} %bitcast.32, f32[512,4]{0,1:T(4,128)S(1)} %compare_convert_fusion, f32[512,64]{0,1:T(8,128)S(1)} %fusion.81), kind=kOutput, calls=%fused_computation.130 | convolution fusion | flops 868291584 | bytes 4900864 | tf_op jit(solution)/shard_map/dot_general | solution.py:119
  148.5 42.2 %all-to-all-done = f32[2,2,128,2048]{3,2,1,0:T(8,128)} async-done(((f32[2,2,128,2048]{3,2,1,0:T(8,128)}), f32[2,2,128,2048]{3,2,1,0:T(8,128)}, u32[]{:S(2)}, u32[]{:S(2)}) %all-to-all-start) | async-done | bytes 4194336 | tf_op jit(solution)/shard_map/all_to_all | solution.py:42
  190.6 2.6 copy.32
  193.3 9.2 %all_to_all.10 = f32[2,2,128,2048]{3,2,0,1:T(8,128)S(1)} all-to-all(f32[2,2,128,2048]{3,2,0,1:T(8,128)S(1)} %copy.32), channel_id=1, replica_groups=mesh['grp_0'=2,'grp_1'=2,'tile'=32] {'grp_1'}, dimensions={1} | all-to-all | bytes 8388608 | tf_op jit(solution)/shard_map/all_to_all | solution.py:42
  203.0 1.7 copy-done.4
  204.7 6.1 %convert_reduce_fusion = (f32[2048]{0:T(1024)S(1)}, bf16[512,2048]{1,0:T(8,128)(2,1)}, f32[512,2048]{1,0:T(8,128)S(1)}) fusion(f32[2,2,128,2048]{3,2,1,0:T(8,128)S(1)} %copy.33, f32[2048]{0:T(1024)S(1)} %copy-done.23, bf16[2048,2048]{1,0:T(8,128)(2,1)S(1)} %bitcast.35, f32[512,2048]{1,0:T(8,128)S(1)} %copy-done.4), kind=kOutput, calls=%fused_computation.121 | convolution fusion | flops 4307548160 | bytes 23085056 | tf_op jit(solution)/shard_map/dot_general | solution.py:122
  210.8 6.1 %fusion.86 = f32[512,2048]{1,0:T(8,128)} fusion(bf16[2048,2048]{1,0:T(8,128)(2,1)S(1)} %bitcast.35, f32[512,2048]{1,0:T(8,128)S(1)} %get-tuple-element.37), kind=kOutput, calls=%fused_computation.164 | convolution fusion | flops 4297064448 | bytes 16777216 | tf_op jit(solution)/shard_map/dot_general | solution.py:133
  216.8 7.0 %fusion.74 = f32[69,2048]{1,0:T(8,128)} fusion(f32[512,2048]{1,0:T(8,128)} %fusion.86, f32[512,2048]{1,0:T(8,128)S(1)} %copy-done.4, f32[512,1]{0,1:T(1,128)S(1)} %bitcast.33, f32[512,4]{0,1:T(4,128)S(1)} %compare_convert_fusion, f32[512,64]{0,1:T(8,128)S(1)} %fusion.81), kind=kOutput, calls=%fused_computation.115 | convolution fusion | flops 876680192 | bytes 9095168 | tf_op jit(solution)/shard_map/dot_general | solution.py:136
  223.9 14.6 %subtract_convert_fusion = bf16[2048,2048]{1,0:T(8,128)(2,1)} fusion(bf16[2048,2048]{1,0:T(8,128)(2,1)} %param.14, f32[512,2048]{1,0:T(8,128)} %copy-done.47, f32[512,2048]{1,0:T(8,128)} %fusion.82), kind=kOutput, calls=%fused_computation | convolution fusion | flops 4319084544 | bytes 25165824 | tf_op jit(solution)/shard_map/dot_general | solution.py:127
  239.1 135.0 %all-reduce.10.cloned.1.call-done = f32[69,2048]{1,0:T(8,128)} async-done(((f32[69,2048]{1,0:T(8,128)}), f32[69,2048]{1,0:T(8,128)}) %all-reduce.10.cloned.1.call-update) | async-done | bytes 565264 | tf_op jit(solution)/shard_map/psum | solution.py:139
  374.0 1.9 multiply_subtract_fusion
  (124 shorter events, 5.8 us)
Async XLA Ops:
  7.2 16.4 %copy-start.22 = (s32[512,8]{0,1:T(8,128)S(1)}, s32[512,8]{0,1:T(8,128)}, u32[]{:S(2)}) copy-start(s32[512,8]{0,1:T(8,128)} %param.10) | copy-start | bytes 49156
  8.0 25.9 %collective-permute-start.2 = (s32[4,512]{1,0:T(4,128)S(1)}, s32[4,512]{1,0:T(4,128)S(1)}, u32[]{:S(2)}, u32[]{:S(2)}) collective-permute-start(s32[4,512]{1,0:T(4,128)S(1)} %get-tuple-element.24), channel_id=1, source_target_pairs={{0,1},{1,2},{2,3},{3,4},{4,5},{5,6},{6,7},{7,8},{8,9},{9,10},{10,1... | collective-permute-start | bytes 24584 | tf_op jit(solution)/shard_map/ppermute | solution.py:20
  12.3 21.6 %collective-permute-start.3 = (s32[4,512]{1,0:T(4,128)S(1)}, s32[4,512]{1,0:T(4,128)S(1)}, u32[]{:S(2)}, u32[]{:S(2)}) collective-permute-start(s32[4,512]{1,0:T(4,128)S(1)} %get-tuple-element.25), channel_id=1, source_target_pairs={{1,0},{2,1},{3,2},{4,3},{5,4},{6,5},{7,6},{8,7},{9,8},{10,9},{11,1... | collective-permute-start | bytes 24584 | tf_op jit(solution)/shard_map/ppermute | solution.py:21
  16.7 32.2 %collective-permute-start = (f32[128,4,512]{2,0,1:T(8,128)S(1)}, f32[128,4,512]{2,0,1:T(8,128)S(1)}, u32[]{:S(2)}, u32[]{:S(2)}) collective-permute-start(f32[128,4,512]{2,0,1:T(8,128)S(1)} %copy.34), channel_id=1, source_target_pairs={{0,1},{1,2},{2,3},{3,4},{4,5},{5,6},{6,7},{7,8},{8,9},{9,10},{10,1... | collective-permute-start | bytes 3145736 | tf_op jit(solution)/shard_map/ppermute | solution.py:20
  22.3 27.0 %collective-permute-start.1 = (f32[128,4,512]{2,0,1:T(8,128)}, f32[128,4,512]{2,0,1:T(8,128)}, u32[]{:S(2)}, u32[]{:S(2)}) collective-permute-start(f32[128,4,512]{2,0,1:T(8,128)} %copy.35), channel_id=1, source_target_pairs={{1,0},{2,1},{3,2},{4,3},{5,4},{6,5},{7,6},{8,7},{9,8},{10,9},{11,1... | collective-permute-start | bytes 3145736 | tf_op jit(solution)/shard_map/ppermute | solution.py:21
  23.6 25.2 %copy-start.24 = (f32[128]{0:T(128)}, f32[128]{0:T(128)S(1)}, u32[]{:S(2)}) copy-start(f32[128]{0:T(128)S(1)} %get-tuple-element.27) | copy-start | bytes 1540
  23.6 25.2 %copy-start.26 = (f32[128]{0:T(128)}, f32[128]{0:T(128)S(1)}, u32[]{:S(2)}) copy-start(f32[128]{0:T(128)S(1)} %get-tuple-element.28) | copy-start | bytes 1540
  23.6 25.2 %copy-start.28 = (f32[128]{0:T(128)}, f32[128]{0:T(128)S(1)}, u32[]{:S(2)}) copy-start(f32[128]{0:T(128)S(1)} %get-tuple-element.29) | copy-start | bytes 1540
  23.6 25.2 %copy-start.30 = (f32[128]{0:T(128)}, f32[128]{0:T(128)S(1)}, u32[]{:S(2)}) copy-start(f32[128]{0:T(128)S(1)} %get-tuple-element.30) | copy-start | bytes 1540
  23.6 25.2 %copy-start.32 = (f32[128]{0:T(128)}, f32[128]{0:T(128)S(1)}, u32[]{:S(2)}) copy-start(f32[128]{0:T(128)S(1)} %get-tuple-element.31) | copy-start | bytes 1540
  23.7 25.2 %copy-start.34 = (f32[128]{0:T(128)}, f32[128]{0:T(128)S(1)}, u32[]{:S(2)}) copy-start(f32[128]{0:T(128)S(1)} %get-tuple-element.32) | copy-start | bytes 1540
  23.7 25.2 %copy-start.36 = (f32[128]{0:T(128)}, f32[128]{0:T(128)S(1)}, u32[]{:S(2)}) copy-start(f32[128]{0:T(128)S(1)} %get-tuple-element.33) | copy-start | bytes 1540
  33.9 15.0 %copy-start.6 = (f32[24,512]{1,0:T(8,128)}, f32[24,512]{1,0:T(8,128)S(1)}, u32[]{:S(2)}) copy-start(f32[24,512]{1,0:T(8,128)S(1)} %get-tuple-element.22) | copy-start | bytes 147460
  33.9 15.0 %copy-start.8 = (f32[24,512]{1,0:T(8,128)}, f32[24,512]{1,0:T(8,128)S(1)}, u32[]{:S(2)}) copy-start(f32[24,512]{1,0:T(8,128)S(1)} %get-tuple-element.23) | copy-start | bytes 147460
  34.0 14.9 %copy-start.10 = (f32[24,512]{1,0:T(8,128)}, f32[24,512]{1,0:T(8,128)S(1)}, u32[]{:S(2)}) copy-start(f32[24,512]{1,0:T(8,128)S(1)} %get-tuple-element.16) | copy-start | bytes 147460
  34.0 14.9 %copy-start.12 = (f32[24,512]{1,0:T(8,128)}, f32[24,512]{1,0:T(8,128)S(1)}, u32[]{:S(2)}) copy-start(f32[24,512]{1,0:T(8,128)S(1)} %get-tuple-element.17) | copy-start | bytes 147460
  34.0 14.9 %copy-start.14 = (f32[24,512]{1,0:T(8,128)}, f32[24,512]{1,0:T(8,128)S(1)}, u32[]{:S(2)}) copy-start(f32[24,512]{1,0:T(8,128)S(1)} %get-tuple-element.18) | copy-start | bytes 147460
  34.0 14.9 %copy-start.16 = (f32[24,512]{1,0:T(8,128)}, f32[24,512]{1,0:T(8,128)S(1)}, u32[]{:S(2)}) copy-start(f32[24,512]{1,0:T(8,128)S(1)} %get-tuple-element.19) | copy-start | bytes 147460
  34.0 14.9 %copy-start.18 = (f32[24,512]{1,0:T(8,128)}, f32[24,512]{1,0:T(8,128)S(1)}, u32[]{:S(2)}) copy-start(f32[24,512]{1,0:T(8,128)S(1)} %get-tuple-element.20) | copy-start | bytes 147460
  34.0 14.9 %copy-start.20 = (f32[24,512]{1,0:T(8,128)}, f32[24,512]{1,0:T(8,128)S(1)}, u32[]{:S(2)}) copy-start(f32[24,512]{1,0:T(8,128)S(1)} %get-tuple-element.21) | copy-start | bytes 147460
  71.1 11.3 %copy-start.46 = (pred[20]{0:T(512)(128)(4,1)S(1)}, pred[20]{0:T(512)(128)(4,1)}, u32[]{:S(2)}) copy-start(pred[20]{0:T(512)(128)(4,1)} %compare_and_fusion.1) | copy-start | bytes 64
  82.4 16.6 %copy-start = (f32[128,22,512]{0,2,1:T(8,128)}, f32[128,22,512]{0,2,1:T(8,128)S(1)}, u32[]{:S(2)}) copy-start(f32[128,22,512]{0,2,1:T(8,128)S(1)} %get-tuple-element.11) | copy-start | bytes 17301508
  82.4 16.7 %copy-start.45 = (pred[18]{0:T(512)(128)(4,1)S(1)}, pred[18]{0:T(512)(128)(4,1)}, u32[]{:S(2)}) copy-start(pred[18]{0:T(512)(128)(4,1)} %compare_and_fusion.2) | copy-start | bytes 58
  99.0 10.9 %copy-start.1 = (f32[128,20,512]{0,2,1:T(8,128)}, f32[128,20,512]{0,2,1:T(8,128)S(1)}, u32[]{:S(2)}) copy-start(f32[128,20,512]{0,2,1:T(8,128)S(1)} %get-tuple-element.9) | copy-start | bytes 15728644
  99.0 10.9 %copy-start.40 = (pred[128]{0:T(512)(128)(4,1)S(1)}, pred[128]{0:T(512)(128)(4,1)}, u32[]{:S(2)}) copy-start(pred[128]{0:T(512)(128)(4,1)} %get-tuple-element.4) | copy-start | bytes 388
  99.0 10.9 %copy-start.41 = (pred[128]{0:T(512)(128)(4,1)S(1)}, pred[128]{0:T(512)(128)(4,1)}, u32[]{:S(2)}) copy-start(pred[128]{0:T(512)(128)(4,1)} %get-tuple-element.34) | copy-start | bytes 388
  99.0 10.9 %copy-start.42 = (pred[128]{0:T(512)(128)(4,1)S(1)}, pred[128]{0:T(512)(128)(4,1)}, u32[]{:S(2)}) copy-start(pred[128]{0:T(512)(128)(4,1)} %get-tuple-element.35) | copy-start | bytes 388
  99.1 10.9 %copy-start.43 = (pred[128]{0:T(512)(128)(4,1)S(1)}, pred[128]{0:T(512)(128)(4,1)}, u32[]{:S(2)}) copy-start(pred[128]{0:T(512)(128)(4,1)} %get-tuple-element.36) | copy-start | bytes 388
  99.1 10.9 %copy-start.44 = (pred[16]{0:T(512)(128)(4,1)S(1)}, pred[16]{0:T(512)(128)(4,1)}, u32[]{:S(2)}) copy-start(pred[16]{0:T(512)(128)(4,1)} %compare_and_fusion.3) | copy-start | bytes 52
  137.3 53.4 %all-to-all-start = ((f32[2,2,128,2048]{3,2,1,0:T(8,128)}), f32[2,2,128,2048]{3,2,1,0:T(8,128)}, u32[]{:S(2)}, u32[]{:S(2)}) async-start(f32[2,2,128,2048]{3,2,1,0:T(8,128)} %bitcast.31), calls=%async_computation | async-start | bytes 8388608 | tf_op jit(solution)/shard_map/all_to_all | solution.py:42
  143.0 231.0 %all-reduce.10.cloned.1.call-start = ((), (), s32[]{:S(2)}) async-start(), calls=%async_computation.2 | async-start | bytes 1179648 | tf_op jit(solution)/shard_map/psum | solution.py:139
  190.6 12.4 %slice-start = ((s8[8388608]{0:T(1024)(128)(4,1)}), s8[4194304]{0:T(1024)(128)(4,1)S(1)}, s32[]{:S(2)}) async-start(s8[8388608]{0:T(1024)(128)(4,1)} %bitcast.34), calls=%async_computation.3 | async-start | bytes 8388608
  (24 other events, 94.4 us)
Sparse Core Ops, SparseCore 0:
  224.0 150.0 all-reduce.9
where the time goes:
time: 384 us; the launch traced here: 383 us
  waiting for transfers between devices  177 us (46%)
  other arithmetic  101 us (26%)
  matrix products  38.8 us (10%)
  local copies, waits for them, and re-layouts  24.5 us (6%)
  starting transfers between devices  17 us (4%)
  between operations  14.8 us (4%)
  blocking collectives  9.24 us (2%)
    psum x1, waiting for transfers between devices, on_device(): grad_in = lax.psum(partial_in, GRP_TILE)  135 us
    div x4, other arithmetic, advance(): spread = kappa * (1.0 + steep * ratio) / (1.0 + ratio)  54.4 us
    all_to_all x1, waiting for transfers between devices, turned_blocks(): out = lax.all_to_all(out, axes[k], k, k, tiled=True)  42.2 us
    select_n x1, other arithmetic, on_device(): jnp.where(pick_here == step + 1, wide[:, margin:margin + rows], snapshot)  21.7 us
    add x1, other arithmetic, coefficients(): kappa = kappa + picked[None] * table[:, klass][:, None, None]  14.8 us
    dot_general x1, matrix products, on_device(): lax.dot_general(hidden, slope, (((0,), (0,)), ((), ())), preferred_elemen...  14.6 us
    unnamed x103, local copies, waits for them, and re-layouts  10.4 us
    all_to_all x1, blocking collectives, turned_blocks(): out = lax.all_to_all(out, axes[k], k, k, tiled=True)  9.24 us
  transfers between devices with their start and end apart: 6, of which 2 were waited for; matrix products, arithmetic and copies ran while one was open for 13% of the time, Pallas kernels for 0%

commit v1 on v0

--- a/solution.py
+++ b/solution.py
@@ -136,7 +136,7 @@
     partial_in = lax.dot_general(
         feats, partial_back * gain_slope, (((0,), (0,)), ((), ())), precision=lax.Precision.HIGHEST
     )
-    grad_in = lax.psum(partial_in, GRP_TILE)
+    grad_in = lax.psum(lax.psum(partial_in, ("grp_1", "tile")), "grp_0")
     input_next = input_layer - 2.0 * grad_in
     return (error.astype(jnp.bfloat16), output_next, bias_next, input_next)
 

time: 384 us -> 841 us (2.19)
  waiting for transfers between devices: 177 us -> 635 us
    psum x1 -> x2, waiting for transfers between devices: 135 us -> 592 us  [on_device(): grad_in = lax.psum(lax.psum(partial_in, ('grp_1', 'tile')), 'grp_0')]
  transfers between devices with their start and end apart: 6 -> 7, of which waited for: 2 -> 3; matrix products, arithmetic and copies ran while one was open for 13% -> 6% of each run, Pallas kernels for 0% -> 0%
where the time goes in v1:
time: 841 us
  waiting for transfers between devices  635 us (76%)
  other arithmetic  101 us (12%)
  matrix products  38.8 us (5%)
  local copies, waits for them, and re-layouts  24.5 us (3%)
  starting transfers between devices  17.3 us (2%)
  between operations  14.8 us (2%)
  blocking collectives  9.24 us (1%)
    psum x2, waiting for transfers between devices, on_device(): grad_in = lax.psum(lax.psum(partial_in, ('grp_1', 'tile')), 'grp_0')  592 us
    div x4, other arithmetic, advance(): spread = kappa * (1.0 + steep * ratio) / (1.0 + ratio)  54.4 us
    all_to_all x1, waiting for transfers between devices, turned_blocks(): out = lax.all_to_all(out, axes[k], k, k, tiled=True)  42.2 us
    select_n x1, other arithmetic, on_device(): jnp.where(pick_here == step + 1, wide[:, margin:margin + rows], snapshot)  21.7 us
  transfers between devices with their start and end apart: 7, of which 3 were waited for; matrix products, arithmetic and copies ran while one was open for 6% of the time, Pallas kernels for 0%

profile of v1, /device:TPU:1, one launch (start us, length us, event | category | flops | bytes accessed | tf_op | source)
XLA Modules:
  0.0 840.6 jit_solution(3473909853904309086)
XLA Ops:
  7.2 0.8 broadcast_add_fusion
  8.0 4.4 collective-permute-start.2
  12.3 1.3 collective-permute-start.3
  13.6 2.7 fusion.90
  16.7 4.2 collective-permute-start
  21.0 1.3 copy.35
  22.3 1.3 collective-permute-start.1
  25.4 1.3 broadcast_compare_fusion.3
  27.8 5.3 copy.29
  34.0 14.8 %multiply_add_fusion = f32[128,24,512]{0,2,1:T(8,128)} fusion(f32[128]{0:T(128)S(1)} %get-tuple-element.27, f32[24,512]{1,0:T(8,128)S(1)} %get-tuple-element.23, f32[128]{0:T(128)S(1)} %get-tuple-element.28, f32[24,512]{1,0:T(8,128)S(1)} %get-tuple-element.22, f32[128]{0:T(128)S(1)} %get-tuple-element.29, f32[24,512]{1,0:T(8,128)S(1)} %get-tuple-element.21, ...), kind=kLoop, calls=%fused_computation.3 | loop fusion | flops 23592960 | bytes 6688768 | tf_op jit(solution)/shard_map/add | solution.py:57
  49.3 1.5 copy.30
  50.9 1.0 copy-done.3
  52.0 2.7 pad_maximum_fusion
  55.4 15.7 %add_divide_fusion = f32[128,24,512]{0,2,1:T(8,128)S(1)} fusion(f32[128]{0:T(128)S(1)} %dynamic_slice.11, f32[128,4,512]{0,2,1:T(8,128)} %copy-done.3, f32[128,16,512]{0,2,1:T(8,128)S(1)} %copy-done.2, f32[128,4,512]{0,2,1:T(8,128)S(1)} %copy.28, f32[128]{0:T(128)S(1)} %copy-done.25, f32[24,512]{1,0:T(8,128)S(1)} %copy-done.9, f32[128]{0:T(128)S(1)} %copy-done.27, ...), kind=kLoop, calls=%fused_computation.2 | loop fusion | flops 36175872 | bytes 12980736 | tf_op jit(solution)/shard_map/div | solution.py:63
  71.1 11.3 %fusion.11 = (f32[128,22,512]{0,2,1:T(8,128)}, f32[128,22,512]{0,2,1:T(8,128)S(1)}) fusion(f32[128,24,512]{0,2,1:T(8,128)} %multiply_add_fusion, f32[128]{0:T(128)S(1)} %dynamic_slice.11, f32[128,24,512]{0,2,1:T(8,128)S(1)} %pad_maximum_fusion, f32[128,24,512]{0,2,1:T(8,128)S(1)} %add_divide_fusion, pred[22]{0:T(512)(128)(4,1)} %compare_and_fusion), kind=kLoop, calls=%fused_computation.20 | loop fusion | flops 38928384 | bytes 64487960 | tf_op jit(solution)/shard_map/div | solution.py:63
  82.4 16.6 %fusion.29 = (f32[128,20,512]{0,2,1:T(8,128)S(1)}, f32[128,20,512]{0,2,1:T(8,128)S(1)}) fusion(f32[128,24,512]{0,2,1:T(8,128)} %multiply_add_fusion, f32[128]{0:T(128)S(1)} %dynamic_slice.11, f32[128,22,512]{0,2,1:T(8,128)S(1)} %get-tuple-element.11, f32[128,22,512]{0,2,1:T(8,128)} %get-tuple-element.10, pred[20]{0:T(512)(128)(4,1)S(1)} %copy-done.46), kind=kLoop, calls=%fused_computation.47 | loop fusion | flops 35389440 | bytes 58721280 | tf_op jit(solution)/shard_map/div | solution.py:63
  99.1 10.9 %fusion.47 = (f32[128,18,512]{0,2,1:T(8,128)}, f32[128,18,512]{0,2,1:T(8,128)}) fusion(f32[128,24,512]{0,2,1:T(8,128)} %multiply_add_fusion, f32[128]{0:T(128)S(1)} %dynamic_slice.11, f32[128,20,512]{0,2,1:T(8,128)S(1)} %get-tuple-element.9, f32[128,20,512]{0,2,1:T(8,128)S(1)} %get-tuple-element.8, pred[18]{0:T(512)(128)(4,1)S(1)} %copy-done.45), kind=kLoop, calls=%fused_computation.74 | loop fusion | flops 31850496 | bytes 52954112 | tf_op jit(solution)/shard_map/div | solution.py:63
  110.0 21.7 %fusion.60 = f32[128,16,512]{0,2,1:T(8,128)} fusion(f32[128,18,512]{0,2,1:T(8,128)} %get-tuple-element.6, f32[128,18,512]{0,2,1:T(8,128)} %get-tuple-element.7, f32[128,22,512]{0,2,1:T(8,128)} %copy-done, f32[128,20,512]{0,2,1:T(8,128)} %copy-done.1, pred[16]{0:T(512)(128)(4,1)S(1)} %copy-done.44, pred[128]{0:T(512)(128)(4,1)S(1)} %copy-done.43, ...), kind=kLoop, calls=%fused_computation.95 | loop fusion | flops 26214400 | bytes 47186448 | tf_op jit(solution)/shard_map/jit(_where)/select_n | solution.py:114
  131.7 5.6 copy.31
  137.3 5.8 all-to-all-start
  143.4 5.1 fusion.82
  148.5 42.2 %all-to-all-done = f32[2,2,128,2048]{3,2,1,0:T(8,128)} async-done(((f32[2,2,128,2048]{3,2,1,0:T(8,128)}), f32[2,2,128,2048]{3,2,1,0:T(8,128)}, u32[]{:S(2)}, u32[]{:S(2)}) %all-to-all-start) | async-done | bytes 4194336 | tf_op jit(solution)/shard_map/all_to_all | solution.py:42
  190.6 2.6 copy.32
  193.3 9.2 %all_to_all.10 = f32[2,2,128,2048]{3,2,0,1:T(8,128)S(1)} all-to-all(f32[2,2,128,2048]{3,2,0,1:T(8,128)S(1)} %copy.32), channel_id=1, replica_groups=mesh['grp_0'=2,'grp_1'=2,'tile'=32] {'grp_1'}, dimensions={1} | all-to-all | bytes 8388608 | tf_op jit(solution)/shard_map/all_to_all | solution.py:42
  203.0 1.7 copy-done.4
  204.7 6.1 convert_reduce_fusion
  210.8 6.1 fusion.86
  216.8 7.0 fusion.74
  224.1 556.1 %all-reduce.11.cloned.1.call-done = f32[69,2048]{1,0:T(8,128)} async-done(((f32[69,2048]{1,0:T(8,128)}), f32[69,2048]{1,0:T(8,128)}) %all-reduce.11.cloned.1.call-update) | async-done | bytes 565264 | tf_op jit(solution)/shard_map/psum | solution.py:139
  780.3 14.6 %subtract_convert_fusion = bf16[2048,2048]{1,0:T(8,128)(2,1)} fusion(bf16[2048,2048]{1,0:T(8,128)(2,1)} %param.14, f32[512,2048]{1,0:T(8,128)} %copy-done.47, f32[512,2048]{1,0:T(8,128)} %fusion.82), kind=kOutput, calls=%fused_computation | convolution fusion | flops 4319084544 | bytes 25165824 | tf_op jit(solution)/shard_map/dot_general | solution.py:127
  795.5 36.3 %all-reduce.13.cloned.1.call-done = f32[69,2048]{1,0:T(8,128)} async-done(((f32[69,2048]{1,0:T(8,128)}), f32[69,2048]{1,0:T(8,128)}) %all-reduce.13.cloned.1.call-update) | async-done | bytes 565264 | tf_op jit(solution)/shard_map/psum | solution.py:139
  831.8 1.9 multiply_subtract_fusion
  (127 shorter events, 6.8 us)
Async XLA Ops:
  7.2 16.4 %copy-start.22 = (s32[512,8]{0,1:T(8,128)S(1)}, s32[512,8]{0,1:T(8,128)}, u32[]{:S(2)}) copy-start(s32[512,8]{0,1:T(8,128)} %param.10) | copy-start | bytes 49156
  8.0 25.9 %collective-permute-start.2 = (s32[4,512]{1,0:T(4,128)S(1)}, s32[4,512]{1,0:T(4,128)S(1)}, u32[]{:S(2)}, u32[]{:S(2)}) collective-permute-start(s32[4,512]{1,0:T(4,128)S(1)} %get-tuple-element.24), channel_id=1, source_target_pairs={{0,1},{1,2},{2,3},{3,4},{4,5},{5,6},{6,7},{7,8},{8,9},{9,10},{10,1... | collective-permute-start | bytes 24584 | tf_op jit(solution)/shard_map/ppermute | solution.py:20
  12.3 21.6 %collective-permute-start.3 = (s32[4,512]{1,0:T(4,128)S(1)}, s32[4,512]{1,0:T(4,128)S(1)}, u32[]{:S(2)}, u32[]{:S(2)}) collective-permute-start(s32[4,512]{1,0:T(4,128)S(1)} %get-tuple-element.25), channel_id=1, source_target_pairs={{1,0},{2,1},{3,2},{4,3},{5,4},{6,5},{7,6},{8,7},{9,8},{10,9},{11,1... | collective-permute-start | bytes 24584 | tf_op jit(solution)/shard_map/ppermute | solution.py:21
  16.7 32.2 %collective-permute-start = (f32[128,4,512]{2,0,1:T(8,128)S(1)}, f32[128,4,512]{2,0,1:T(8,128)S(1)}, u32[]{:S(2)}, u32[]{:S(2)}) collective-permute-start(f32[128,4,512]{2,0,1:T(8,128)S(1)} %copy.34), channel_id=1, source_target_pairs={{0,1},{1,2},{2,3},{3,4},{4,5},{5,6},{6,7},{7,8},{8,9},{9,10},{10,1... | collective-permute-start | bytes 3145736 | tf_op jit(solution)/shard_map/ppermute | solution.py:20
  22.3 27.0 %collective-permute-start.1 = (f32[128,4,512]{2,0,1:T(8,128)}, f32[128,4,512]{2,0,1:T(8,128)}, u32[]{:S(2)}, u32[]{:S(2)}) collective-permute-start(f32[128,4,512]{2,0,1:T(8,128)} %copy.35), channel_id=1, source_target_pairs={{1,0},{2,1},{3,2},{4,3},{5,4},{6,5},{7,6},{8,7},{9,8},{10,9},{11,1... | collective-permute-start | bytes 3145736 | tf_op jit(solution)/shard_map/ppermute | solution.py:21
  23.6 25.2 %copy-start.24 = (f32[128]{0:T(128)}, f32[128]{0:T(128)S(1)}, u32[]{:S(2)}) copy-start(f32[128]{0:T(128)S(1)} %get-tuple-element.27) | copy-start | bytes 1540
  23.6 25.2 %copy-start.26 = (f32[128]{0:T(128)}, f32[128]{0:T(128)S(1)}, u32[]{:S(2)}) copy-start(f32[128]{0:T(128)S(1)} %get-tuple-element.28) | copy-start | bytes 1540
  23.6 25.2 %copy-start.28 = (f32[128]{0:T(128)}, f32[128]{0:T(128)S(1)}, u32[]{:S(2)}) copy-start(f32[128]{0:T(128)S(1)} %get-tuple-element.29) | copy-start | bytes 1540
  23.6 25.2 %copy-start.30 = (f32[128]{0:T(128)}, f32[128]{0:T(128)S(1)}, u32[]{:S(2)}) copy-start(f32[128]{0:T(128)S(1)} %get-tuple-element.30) | copy-start | bytes 1540
  23.6 25.2 %copy-start.32 = (f32[128]{0:T(128)}, f32[128]{0:T(128)S(1)}, u32[]{:S(2)}) copy-start(f32[128]{0:T(128)S(1)} %get-tuple-element.31) | copy-start | bytes 1540
  23.7 25.2 %copy-start.34 = (f32[128]{0:T(128)}, f32[128]{0:T(128)S(1)}, u32[]{:S(2)}) copy-start(f32[128]{0:T(128)S(1)} %get-tuple-element.32) | copy-start | bytes 1540
  23.7 25.2 %copy-start.36 = (f32[128]{0:T(128)}, f32[128]{0:T(128)S(1)}, u32[]{:S(2)}) copy-start(f32[128]{0:T(128)S(1)} %get-tuple-element.33) | copy-start | bytes 1540
  33.9 15.0 %copy-start.6 = (f32[24,512]{1,0:T(8,128)}, f32[24,512]{1,0:T(8,128)S(1)}, u32[]{:S(2)}) copy-start(f32[24,512]{1,0:T(8,128)S(1)} %get-tuple-element.22) | copy-start | bytes 147460
  33.9 15.0 %copy-start.8 = (f32[24,512]{1,0:T(8,128)}, f32[24,512]{1,0:T(8,128)S(1)}, u32[]{:S(2)}) copy-start(f32[24,512]{1,0:T(8,128)S(1)} %get-tuple-element.23) | copy-start | bytes 147460
  34.0 14.9 %copy-start.10 = (f32[24,512]{1,0:T(8,128)}, f32[24,512]{1,0:T(8,128)S(1)}, u32[]{:S(2)}) copy-start(f32[24,512]{1,0:T(8,128)S(1)} %get-tuple-element.16) | copy-start | bytes 147460
  34.0 14.9 %copy-start.12 = (f32[24,512]{1,0:T(8,128)}, f32[24,512]{1,0:T(8,128)S(1)}, u32[]{:S(2)}) copy-start(f32[24,512]{1,0:T(8,128)S(1)} %get-tuple-element.17) | copy-start | bytes 147460
  34.0 14.9 %copy-start.14 = (f32[24,512]{1,0:T(8,128)}, f32[24,512]{1,0:T(8,128)S(1)}, u32[]{:S(2)}) copy-start(f32[24,512]{1,0:T(8,128)S(1)} %get-tuple-element.18) | copy-start | bytes 147460
  34.0 14.9 %copy-start.16 = (f32[24,512]{1,0:T(8,128)}, f32[24,512]{1,0:T(8,128)S(1)}, u32[]{:S(2)}) copy-start(f32[24,512]{1,0:T(8,128)S(1)} %get-tuple-element.19) | copy-start | bytes 147460
  34.0 14.9 %copy-start.18 = (f32[24,512]{1,0:T(8,128)}, f32[24,512]{1,0:T(8,128)S(1)}, u32[]{:S(2)}) copy-start(f32[24,512]{1,0:T(8,128)S(1)} %get-tuple-element.20) | copy-start | bytes 147460
  34.0 14.9 %copy-start.20 = (f32[24,512]{1,0:T(8,128)}, f32[24,512]{1,0:T(8,128)S(1)}, u32[]{:S(2)}) copy-start(f32[24,512]{1,0:T(8,128)S(1)} %get-tuple-element.21) | copy-start | bytes 147460
  71.1 11.3 %copy-start.46 = (pred[20]{0:T(512)(128)(4,1)S(1)}, pred[20]{0:T(512)(128)(4,1)}, u32[]{:S(2)}) copy-start(pred[20]{0:T(512)(128)(4,1)} %compare_and_fusion.1) | copy-start | bytes 64
  82.4 16.6 %copy-start = (f32[128,22,512]{0,2,1:T(8,128)}, f32[128,22,512]{0,2,1:T(8,128)S(1)}, u32[]{:S(2)}) copy-start(f32[128,22,512]{0,2,1:T(8,128)S(1)} %get-tuple-element.11) | copy-start | bytes 17301508
  82.4 16.7 %copy-start.45 = (pred[18]{0:T(512)(128)(4,1)S(1)}, pred[18]{0:T(512)(128)(4,1)}, u32[]{:S(2)}) copy-start(pred[18]{0:T(512)(128)(4,1)} %compare_and_fusion.2) | copy-start | bytes 58
  99.0 10.9 %copy-start.1 = (f32[128,20,512]{0,2,1:T(8,128)}, f32[128,20,512]{0,2,1:T(8,128)S(1)}, u32[]{:S(2)}) copy-start(f32[128,20,512]{0,2,1:T(8,128)S(1)} %get-tuple-element.9) | copy-start | bytes 15728644
  99.0 10.9 %copy-start.40 = (pred[128]{0:T(512)(128)(4,1)S(1)}, pred[128]{0:T(512)(128)(4,1)}, u32[]{:S(2)}) copy-start(pred[128]{0:T(512)(128)(4,1)} %get-tuple-element.4) | copy-start | bytes 388
  99.0 10.9 %copy-start.41 = (pred[128]{0:T(512)(128)(4,1)S(1)}, pred[128]{0:T(512)(128)(4,1)}, u32[]{:S(2)}) copy-start(pred[128]{0:T(512)(128)(4,1)} %get-tuple-element.34) | copy-start | bytes 388
  99.0 10.9 %copy-start.42 = (pred[128]{0:T(512)(128)(4,1)S(1)}, pred[128]{0:T(512)(128)(4,1)}, u32[]{:S(2)}) copy-start(pred[128]{0:T(512)(128)(4,1)} %get-tuple-element.35) | copy-start | bytes 388
  99.1 10.9 %copy-start.43 = (pred[128]{0:T(512)(128)(4,1)S(1)}, pred[128]{0:T(512)(128)(4,1)}, u32[]{:S(2)}) copy-start(pred[128]{0:T(512)(128)(4,1)} %get-tuple-element.36) | copy-start | bytes 388
  137.3 53.4 %all-to-all-start = ((f32[2,2,128,2048]{3,2,1,0:T(8,128)}), f32[2,2,128,2048]{3,2,1,0:T(8,128)}, u32[]{:S(2)}, u32[]{:S(2)}) async-start(f32[2,2,128,2048]{3,2,1,0:T(8,128)} %bitcast.31), calls=%async_computation | async-start | bytes 8388608 | tf_op jit(solution)/shard_map/all_to_all | solution.py:42
  143.0 637.2 %all-reduce.11.cloned.1.call-start = ((), (), s32[]{:S(2)}) async-start(), calls=%async_computation.2 | async-start | bytes 1179648 | tf_op jit(solution)/shard_map/psum | solution.py:139
  190.6 12.4 %slice-start = ((s8[8388608]{0:T(1024)(128)(4,1)}), s8[4194304]{0:T(1024)(128)(4,1)S(1)}, s32[]{:S(2)}) async-start(s8[8388608]{0:T(1024)(128)(4,1)} %bitcast.34), calls=%async_computation.4 | async-start | bytes 8388608
  223.9 607.9 %all-reduce.13.cloned.1.call-start = ((), (), s32[]{:S(2)}) async-start(), calls=%async_computation.3 | async-start | bytes 1179648 | tf_op jit(solution)/shard_map/psum | solution.py:139
  (25 other events, 105.3 us)
Sparse Core Ops, SparseCore 0:
  224.0 556.2 all-reduce.10
  782.9 48.8 all-reduce.12
